TPU v7x, 256 devices: a whole 4x4x8 slice. The times are simulated.
256 devices in a mesh: user: 32 (over y, z), hist: 8 (over x, core).
Axes of the slice: x: 4, y: 4, z: 8, core: 2. Of those that a mesh axis runs over, the one named last changes fastest.
Arguments:
- quot_ids: int32 [64, 2048], P('user', 'hist'), may hold values from 0 to 2047
- rem_ids: int32 [64, 2048], P('user', 'hist'), may hold values from 0 to 65535, as said below
- lengths: int32 [64], P('user'), may hold values from 426 to 2048, as said below
- log_decay: float32 [64, 4, 2048], P('user', None, 'hist'), may hold values from -1.1 to 0
- quot_table: bfloat16 [2048, 256], replicated, may hold values from -6 to 6
- rem_table: bfloat16 [65536, 256], P('user'), may hold values from -6 to 6
- w_query: bfloat16 [256, 256], replicated, may hold values from -0.375 to 0.375
- w_key: bfloat16 [256, 256], replicated, may hold values from -0.375 to 0.375
- w_value: bfloat16 [256, 256], replicated, may hold values from -0.375 to 0.375
- w_out: bfloat16 [256, 256], replicated, may hold values from -0.375 to 0.375
- cotangent: bfloat16 [64, 2048, 256], P('user', 'hist'), may hold values from -0.59765625 to 0.59765625
Outputs:
- output: bfloat16 [64, 2048, 256], P('user', 'hist')
- quot_grad: float32 [2048, 256], replicated
- rem_grad: float32 [65536, 256], P('user')
Inputs may be any that keep to these rules, and one draw needn't show every extreme that they name: rem_ids[u, t] // 2048 names a shard of the remainder table. In each aligned block of 256 events of one user (events b * 256 to (b + 1) * 256 - 1), no shard is named by more than 16 events, and one shard, the same for all blocks, is named by exactly 16. The valid events of user u are its first lengths[u] ones.
All inputs are finite; a program needn't handle non-finite values.
Results may differ from a plain program's by a relative error of at most 0.0073.
Values may be sent and summed in bfloat16 or wider, within the bound.
No kernel may reach another device: no remote copies, remote signals or barrier semaphores. Data moves between devices by JAX's collectives and lax.ppermute only.
A program may use at most 192 MiB of HBM per device.

v0:
```python
import math
import jax
import jax.numpy as jnp
from jax import lax
from jax.sharding import PartitionSpec as P

largest_value = lax.Precision.HIGHEST


def carried_in(part, axis, combine, identity):
    place = lax.axis_index(axis)
    gathered = jax.tree.map(lambda a: lax.all_gather(a, axis), part)
    state = jax.tree.map(lambda a, e: jnp.zeros_like(a) + jnp.asarray(e, a.dtype), part, identity)

    def one(step, state):
        return combine(
            state, jax.tree.map(lambda a: lax.dynamic_index_in_dim(a, step, 0, False), gathered)
        )

    return lax.fori_loop(0, place, one, state)


def carried_in_2(shard, axis, combine, identity):
    peers, place = (lax.axis_size(axis), lax.axis_index(axis))
    everything = jax.tree.map(
        lambda part, kind: lax.all_gather(part.astype(kind), axis),
        shard,
        (jnp.bfloat16, jnp.bfloat16),
    )
    start = jax.tree.map(
        lambda part, zero: jnp.broadcast_to(jnp.asarray(zero, part.dtype), part.shape),
        shard,
        identity,
    )

    def step(k, before):
        at = peers - 1 - k
        reached = at > place
        new = combine(
            before, jax.tree.map(lambda part, own: part[at].astype(own.dtype), everything, shard)
        )
        return jax.tree.map(lambda a, b: jnp.where(reached, a, b), new, before)

    return lax.fori_loop(0, peers, step, start)


def decay_mask(cumulative):
    length = cumulative.shape[-1]
    gap = cumulative[..., :, None] - cumulative[..., None, :]
    lower_tri = jnp.arange(length)[:, None] >= jnp.arange(length)[None, :]
    return jnp.where(lower_tri, jnp.exp(jnp.minimum(gap, 0.0)), 0.0)


def link_states(earlier, following):
    return (earlier[0] * following[0], following[0][..., None, None] * earlier[1] + following[1])


def body(
    quot_ids,
    rem_ids,
    lengths,
    log_decay,
    quot_table,
    rem_table,
    w_query,
    w_key,
    w_value,
    w_out,
    cotangent,
):
    user_count, block_len = quot_ids.shape
    feature_width = quot_table.shape[1]
    head_count = log_decay.shape[1]
    head_size = feature_width // head_count
    shards = lax.axis_size("user")
    hist_dev = lax.axis_size("hist")
    rows_own = rem_table.shape[0]
    capacity = 2 * block_len // shards
    history = block_len * hist_dev
    score_scale = 1.0 / math.sqrt(head_size * history)
    slot_total = float(user_count * shards * history)
    own_events = jnp.sum(lengths.astype(jnp.float32))
    all_events = lax.psum(own_events, "user")
    grad_ratio = slot_total / all_events
    flat_ids = rem_ids.reshape(-1)
    owners = flat_ids // rows_own
    matches = (
        owners.reshape(user_count, block_len)[..., None] == jnp.arange(shards, dtype=jnp.int32)
    ).astype(jnp.int32)
    before = jnp.cumsum(matches, axis=1) - matches
    ranking = jnp.sum(before * matches, axis=-1).reshape(-1)
    user_of = jnp.repeat(jnp.arange(user_count, dtype=jnp.int32), block_len)
    slot_index = (owners * user_count + user_of) * capacity + ranking
    requests = (
        jnp.full((shards * user_count * capacity,), -1, jnp.int32).at[slot_index].set(flat_ids)
    )
    requests = requests.reshape(shards, user_count * capacity)
    base_row = lax.axis_index("user") * rows_own
    wanted = lax.all_to_all(requests, "user", split_axis=0, concat_axis=0, tiled=True)
    present = wanted >= 0
    local_row = jnp.where(present, wanted - base_row, 0)
    found_rows = jnp.where(present[..., None], rem_table[local_row], jnp.zeros((), jnp.bfloat16))
    answered = lax.all_to_all(found_rows, "user", split_axis=0, concat_axis=0, tiled=True)
    rem_emb = answered.reshape(-1, feature_width)[slot_index]
    quot_emb = quot_table[quot_ids.reshape(-1)]
    embedded = (quot_emb.astype(jnp.float32) * rem_emb.astype(jnp.float32)).astype(jnp.bfloat16)

    def project(matrix):
        result = jnp.dot(embedded, matrix, preferred_element_type=jnp.float32).astype(jnp.bfloat16)
        return result.reshape(user_count, block_len, head_count, head_size)

    query_rows = project(w_query)
    key_rows = project(w_key)
    value_rows = project(w_value)
    cumulative = jnp.cumsum(log_decay, axis=-1)
    block_end = cumulative[..., -1]
    decay_all = jnp.exp(block_end)
    growth = jnp.exp(cumulative).transpose(0, 2, 1)[..., None]
    falloff = jnp.exp(block_end[..., None] - cumulative).transpose(0, 2, 1)[..., None]
    local_state = jnp.einsum(
        "ulhd,ulhe->uhde",
        key_rows.astype(jnp.float32) * falloff,
        value_rows.astype(jnp.float32),
        precision=largest_value,
    )
    entering = carried_in(
        (decay_all, local_state),
        "hist",
        link_states,
        (jnp.ones_like(decay_all), jnp.zeros_like(local_state)),
    )[1]

    def forward_user(inputs):
        single_query, single_key, single_value, cum_one, grow_one, state_one = inputs
        score_matrix = jnp.einsum(
            "tbc,xbc->btx", single_query, single_key, preferred_element_type=jnp.float32
        )
        weight_matrix = (score_scale * score_matrix * decay_mask(cum_one)).astype(jnp.bfloat16)
        within_bounds = jnp.einsum(
            "tov,vtp->otp", weight_matrix, single_value, preferred_element_type=jnp.float32
        )
        carried = score_scale * jnp.einsum(
            "lhd,hde->lhe",
            single_query.astype(jnp.float32) * grow_one,
            state_one,
            precision=largest_value,
        )
        return ((within_bounds + carried).astype(jnp.bfloat16), weight_matrix)

    mixed, weight_matrix = lax.map(
        forward_user, (query_rows, key_rows, value_rows, cumulative, growth, entering)
    )
    output = jnp.dot(
        mixed.reshape(-1, feature_width), w_out, preferred_element_type=jnp.float32
    ).astype(jnp.bfloat16)
    output = output.reshape(user_count, block_len, feature_width)
    position = lax.axis_index("hist") * block_len + jnp.arange(block_len, dtype=jnp.int32)
    in_history = position[None, :] < lengths[:, None]
    masked_cot = jnp.where(in_history[..., None], cotangent.astype(jnp.float32), 0.0).astype(
        jnp.bfloat16
    )
    dmixed = jnp.dot(
        masked_cot.reshape(-1, feature_width), w_out.T, preferred_element_type=jnp.float32
    ).astype(jnp.bfloat16)
    dmixed = dmixed.reshape(user_count, block_len, head_count, head_size)
    local_grad = jnp.einsum(
        "ulhd,ulhe->uhde",
        query_rows.astype(jnp.float32) * growth,
        dmixed.astype(jnp.float32),
        precision=largest_value,
    )
    leaving = carried_in_2(
        (decay_all, local_grad),
        "hist",
        link_states,
        (jnp.ones_like(decay_all), jnp.zeros_like(local_grad)),
    )[1]

    def backward_user(inputs):
        (
            single_query,
            single_key,
            single_value,
            dmixed_one,
            cum_one,
            grow_one,
            fall_one,
            weight_one,
            state_one,
            leaving_single,
        ) = inputs
        dscores = jnp.einsum(
            "lhe,mhe->hlm", dmixed_one, single_value, preferred_element_type=jnp.float32
        )
        weight_gradient = (score_scale * dscores * decay_mask(cum_one)).astype(jnp.bfloat16)
        dquery = jnp.einsum(
            "tov,vtp->otp", weight_gradient, single_key, preferred_element_type=jnp.float32
        ) + score_scale * grow_one * jnp.einsum(
            "hde,lhe->lhd", state_one, dmixed_one.astype(jnp.float32), precision=largest_value
        )
        dkeys = jnp.einsum(
            "euq,uex->qex", weight_gradient, single_query, preferred_element_type=jnp.float32
        ) + score_scale * fall_one * jnp.einsum(
            "kcg,wkg->wkc",
            leaving_single,
            single_value.astype(jnp.float32),
            precision=largest_value,
        )
        dvalue = jnp.einsum(
            "hlm,lhe->mhe", weight_one, dmixed_one, preferred_element_type=jnp.float32
        ) + score_scale * fall_one * jnp.einsum(
            "zxr,czx->czr", leaving_single, single_key.astype(jnp.float32), precision=largest_value
        )
        return (
            dquery.astype(jnp.bfloat16),
            dkeys.astype(jnp.bfloat16),
            dvalue.astype(jnp.bfloat16),
        )

    dquery, dkeys, dvalue = lax.map(
        backward_user,
        (
            query_rows,
            key_rows,
            value_rows,
            dmixed,
            cumulative,
            growth,
            falloff,
            weight_matrix,
            entering,
            leaving,
        ),
    )
    dembedded = jnp.dot(
        dquery.reshape(-1, feature_width), w_query.T, preferred_element_type=jnp.float32
    )
    dembedded = dembedded + jnp.dot(
        dkeys.reshape(-1, feature_width), w_key.T, preferred_element_type=jnp.float32
    )
    dembedded = dembedded + jnp.dot(
        dvalue.reshape(-1, feature_width), w_value.T, preferred_element_type=jnp.float32
    )
    quot_part = jax.ops.segment_sum(
        dembedded * rem_emb.astype(jnp.float32),
        quot_ids.reshape(-1),
        num_segments=quot_table.shape[0],
    )
    event_terms = dembedded * quot_emb.astype(jnp.float32)
    rem_send = (
        jnp.zeros((shards * user_count * capacity, feature_width), jnp.float32)
        .at[slot_index]
        .set(event_terms)
    )
    rem_send = rem_send.reshape(shards, user_count * capacity, feature_width)
    rem_back = lax.all_to_all(rem_send, "user", split_axis=0, concat_axis=0, tiled=True)
    present_ids = wanted >= 0
    local_rows = jnp.where(present_ids, wanted - base_row, 0).reshape(-1)
    rem_part = jax.ops.segment_sum(
        rem_back.reshape(-1, feature_width), local_rows, num_segments=rows_own
    )
    quot_part = grad_ratio * quot_part
    rem_part = grad_ratio * rem_part
    quot_grad = lax.psum(quot_part, ("user", "hist"))
    rem_grad = lax.psum(rem_part, "hist")
    return (output, quot_grad, rem_grad)


def solution(mesh):
    return jax.shard_map(
        body,
        mesh=mesh,
        in_specs=(
            P("user", "hist"),
            P("user", "hist"),
            P("user"),
            P("user", None, "hist"),
            P(),
            P("user", None),
            P(),
            P(),
            P(),
            P(),
            P("user", "hist", None),
        ),
        out_specs=(P("user", "hist", None), P(), P("user", None)),
        check_vma=False,
    )
```

profile of v0, /device:TPU:8, one launch (start us, length us, event | category | flops | bytes accessed | tf_op | source)
XLA Modules:
  0.0 589.0 jit_solution(10004334027409384725)
XLA Ops:
  7.2 0.8 and_select_fusion.1
  8.0 0.7 copy.124
  8.7 0.7 copy.121
  9.4 1.2 reduce-window.14
  11.0 2.4 scatter_custom_fusion
  13.4 0.7 all_to_all.12
  14.1 11.7 %all-to-all-start = ((s32[32,1,32]{2,1,0:T(1,128)}), s32[32,1,32]{2,1,0:T(1,128)S(1)}, u32[]{:S(2)}, u32[]{:S(2)}) async-start(s32[32,1,32]{2,1,0:T(1,128)} %all_to_all.12), calls=%async_computation | async-start | bytes 32768 | tf_op jit(solution)/shard_map/all_to_all | solution.py:99
  25.8 0.7 reshape.410
  26.5 2.4 reduce-window.16
  29.6 0.7 fusion.87
  30.3 4.1 all-to-all-done
  35.1 3.9 gather_fusion.1
  39.0 1.0 broadcast_select_fusion
  40.0 5.7 all-to-all-start.1
  45.9 10.6 %all-gather.3 = bf16[16,4,1]{1,2,0:T(2,128)(2,1)S(1)} all-gather(bf16[2,4,1]{1,2,0:T(2,128)(2,1)S(1)} %get-tuple-element.494), channel_id=5, replica_groups=mesh['user'=32,'hist'=8] {'hist'}, dimensions={0}, use_global_device_ids=true | all-gather | bytes 144 | tf_op jit(solution)/shard_map/all_gather | solution.py:26
  59.2 3.0 gather_fusion
  62.2 8.9 %all-gather = f32[16,4,1]{1,2,0:T(1,128)} all-gather(f32[2,4,1]{1,2,0:T(1,128)S(1)} %get-tuple-element.495), channel_id=2, replica_groups=mesh['user'=32,'hist'=8] {'hist'}, dimensions={0}, use_global_device_ids=true | all-gather | bytes 288 | tf_op jit(solution)/shard_map/all_gather | solution.py:12
  71.1 2.0 gather_fusion.2
  73.6 0.9 convert_multiply_fusion.5
  74.5 1.1 convolution_convert_fusion.2
  75.6 0.8 copy.88
  76.4 1.0 reshape.409
  77.5 1.7 convert_multiply_fusion.6
  79.2 1.1 convolution_convert_fusion.4
  80.3 1.0 reshape.489
  81.3 1.2 copy.95
  82.6 2.1 fusion.79
  85.1 14.8 %all-gather.2 = bf16[16,4,64,64]{3,2,1,0:T(8,128)(2,1)} all-gather(bf16[2,4,64,64]{3,2,1,0:T(8,128)(2,1)S(1)} %convolution_convert_fusion.5), channel_id=4, replica_groups=mesh['user'=32,'hist'=8] {'hist'}, dimensions={0}, use_global_device_ids=true | all-gather | bytes 589824 | tf_op jit(solution)/shard_map/all_gather | solution.py:26
  99.9 13.4 %while.57 = (s32[]{:T(128)}, f32[2,4,64,64]{3,2,1,0:T(8,128)S(1)}, s32[]{:T(128)}, bf16[8,2,4]{2,1,0:T(2,128)(2,1)}, bf16[8,2,4,64,64]{4,3,2,1,0:T(8,128)(2,1)},...) while((s32[]{:T(128)}, f32[2,4,64,64]{3,2,1,0:T(8,128)S(1)}, s32[]{:T(128)}, ...), condition=%wide.region_13.14_spmd.clone, body=%wide.region_12.13_spmd.clone.sunk | while | flops 163856 | bytes 327935 | solution.py:44
  100.6 1.0 fusion.168
  102.3 1.0 fusion.168
  104.0 1.0 fusion.168
  105.7 1.0 fusion.168
  106.7 0.7 bitcast_convert_fusion.2
  107.4 1.0 fusion.168
  109.1 1.0 fusion.168
  110.7 1.0 fusion.168
  112.4 1.0 fusion.168
  113.7 4.2 while.55
  113.7 1.3 bitcast_dynamic-update-slice_fusion.2
  115.8 1.3 bitcast_dynamic-update-slice_fusion.2
  117.9 0.7 copy-done.7
  118.6 0.7 broadcast.273
  119.3 9.1 %while.56 = (s32[]{:T(128)}, bf16[2,256,4,64]{1,3,2,0:T(8,128)(2,1)}, bf16[2,256,4,64]{1,3,2,0:T(8,128)(2,1)S(1)}, bf16[2,256,4,64]{1,3,2,0:T(8,128)(2,1)S(1)}, ...) while((s32[]{:T(128)}, ...), condition=%wide.region_15.16_spmd, body=%wide.region_14.15_spmd.sunk | while | flops 287442944 | bytes 7786197 | solution.py:220
  119.3 0.7 multiply_bitcast_fusion.3
  120.7 1.3 fusion.167
  123.2 0.7 copy-done.6
  123.9 0.7 multiply_bitcast_fusion.3
  125.2 1.3 fusion.167
  127.8 0.7 copy-done.6
  128.8 1.2 copy.108
  131.3 3.5 scatter_custom_fusion.2
  134.8 9.8 %all-to-all-start.2 = ((f32[32,32,256]{2,1,0:T(8,128)}), f32[32,32,256]{2,1,0:T(8,128)}, u32[]{:S(2)}, u32[]{:S(2)}) async-start(f32[32,32,256]{2,1,0:T(8,128)} %bitcast.331), calls=%async_computation.2 | async-start | bytes 2097152 | tf_op jit(solution)/shard_map/all_to_all | solution.py:256
  145.3 79.2 %psum.21 = f32[]{:T(128)} all-reduce(f32[]{:T(128)} %convert_reduce_fusion), channel_id=1, replica_groups=mesh['user'=32,'hist'=8] {'user'}, use_global_device_ids=true, to_apply=%region_11.12 | all-reduce | flops 1 | bytes 8 | tf_op jit(solution)/shard_map/psum | solution.py:83
  225.1 4.3 scatter_custom_fusion.1
  229.5 1.5 broadcast_multiply_fusion.1
  231.7 7.0 %scatter_custom_fusion.3 = f32[2048,256]{1,0:T(8,128)S(1)} fusion(s32[1024]{0:T(1024)S(1)} %reshape.473, f32[1024,256]{1,0:T(8,128)} %bitcast.52, f32[]{:T(128)} %constant.162.clone.1), kind=kCustom, calls=%fused_computation.108 | custom fusion | flops 262144 | bytes 2097664 | tf_op jit(solution)/shard_map/scatter-add | solution.py:259
  238.8 1.5 broadcast_multiply_fusion
  240.3 0.9 copy-done.8
  241.5 1.0 convolution_convert_fusion.1
  242.5 262.9 %all-reduce.3.cloned.1.call-done = f32[2048,256]{1,0:T(8,128)} async-done(((f32[2048,256]{1,0:T(8,128)}), f32[2048,256]{1,0:T(8,128)}) %all-reduce.3.cloned.1.call-update) | async-done | bytes 2097168 | tf_op jit(solution)/shard_map/psum | solution.py:264
  505.4 72.6 %all-reduce.5.cloned.1.call-done = f32[2048,256]{1,0:T(8,128)} async-done(((f32[2048,256]{1,0:T(8,128)}), f32[2048,256]{1,0:T(8,128)}) %all-reduce.5.cloned.1.call-update) | async-done | bytes 2097168 | tf_op jit(solution)/shard_map/psum | solution.py:265
  578.0 3.2 copy.177
  581.2 1.3 copy.178
  (147 shorter events, 18.7 us)
Async XLA Ops:
  7.2 27.9 %copy-start = (bf16[2048,256]{1,0:T(8,128)(2,1)S(1)}, bf16[2048,256]{1,0:T(8,128)(2,1)}, u32[]{:S(2)}) copy-start(bf16[2048,256]{1,0:T(8,128)(2,1)} %param.24) | copy-start | bytes 3145732
  11.0 60.1 %copy-start.18 = (s32[512,1]{0,1:T(1,128)}, s32[512,1]{0,1:T(1,128)S(1)}, u32[]{:S(2)}) copy-start(s32[512,1]{0,1:T(1,128)S(1)} %compare_select_fusion.1) | copy-start | bytes 6148
  14.1 20.3 %all-to-all-start = ((s32[32,1,32]{2,1,0:T(1,128)}), s32[32,1,32]{2,1,0:T(1,128)S(1)}, u32[]{:S(2)}, u32[]{:S(2)}) async-start(s32[32,1,32]{2,1,0:T(1,128)} %all_to_all.12), calls=%async_computation | async-start | bytes 32768 | tf_op jit(solution)/shard_map/all_to_all | solution.py:99
  39.0 6.8 %copy-start.19 = (s32[2]{0:T(128)S(1)}, s32[2]{0:T(128)}, u32[]{:S(2)}) copy-start(s32[2]{0:T(128)} %param.21) | copy-start | bytes 28
  39.0 6.9 %copy-start.16 = (s32[2,256]{1,0:T(2,128)S(1)}, s32[2,256]{1,0:T(2,128)}, u32[]{:S(2)}) copy-start(s32[2,256]{1,0:T(2,128)} %param.19) | copy-start | bytes 6148
  39.0 19.2 %copy-start.14 = (bf16[2,256,256]{2,1,0:T(8,128)(2,1)S(1)}, bf16[2,256,256]{2,1,0:T(8,128)(2,1)}, u32[]{:S(2)}) copy-start(bf16[2,256,256]{2,1,0:T(8,128)(2,1)} %param.29) | copy-start | bytes 786436
  39.0 19.4 %copy-start.10 = (bf16[256,256]{1,0:T(8,128)(2,1)S(1)}, bf16[256,256]{1,0:T(8,128)(2,1)}, u32[]{:S(2)}) copy-start(bf16[256,256]{1,0:T(8,128)(2,1)} %param.28) | copy-start | bytes 393220
  40.0 31.0 %all-to-all-start.1 = ((bf16[32,32,256]{2,1,0:T(8,128)(2,1)}), bf16[32,32,256]{2,1,0:T(8,128)(2,1)S(1)}, u32[]{:S(2)}, u32[]{:S(2)}) async-start(bf16[32,32,256]{2,1,0:T(8,128)(2,1)} %broadcast_select_fusion), calls=%async_computation.1 | async-start | bytes 1048576 | tf_op jit(solution)/shard_map/all_to_all | solution.py:103
  45.8 67.6 %all-gather.6.cloned.1.call-start = ((), (), s32[]{:S(2)}) async-start(), calls=%async_computation.5 | async-start | bytes 2359296 | tf_op jit(solution)/shard_map/all_gather | solution.py:12
  59.2 13.9 %copy-start.9 = (bf16[256,256]{1,0:T(8,128)(2,1)S(1)}, bf16[256,256]{1,0:T(8,128)(2,1)}, u32[]{:S(2)}) copy-start(bf16[256,256]{1,0:T(8,128)(2,1)} %param.25) | copy-start | bytes 393220
  73.1 6.1 %copy-start.1 = (bf16[512,256]{1,0:T(8,128)(2,1)}, bf16[512,256]{1,0:T(8,128)(2,1)S(1)}, u32[]{:S(2)}) copy-start(bf16[512,256]{1,0:T(8,128)(2,1)S(1)} %gather_fusion.2) | copy-start | bytes 786436
  117.9 0.7 copy-start.7
  121.9 1.0 copy-start.5
  123.2 0.7 copy-start.6
  126.5 1.0 copy-start.5
  127.8 0.7 copy-start.6
  128.5 2.2 copy-start.12
  130.0 0.9 copy-start.13
  131.2 93.9 %copy-start.3 = (f32[512,256]{1,0:T(8,128)}, f32[512,256]{1,0:T(8,128)S(1)}, u32[]{:S(2)}) copy-start(f32[512,256]{1,0:T(8,128)S(1)} %convolution_add_fusion) | copy-start | bytes 1572868
  131.3 13.5 %copy-start.20 = (s32[2]{0:T(128)S(1)}, s32[2]{0:T(128)}, u32[]{:S(2)}) copy-start(s32[2]{0:T(128)} %param.21) | copy-start | bytes 28
  131.3 93.2 %copy-start.17 = (s32[2,256]{1,0:T(2,128)S(1)}, s32[2,256]{1,0:T(2,128)}, u32[]{:S(2)}) copy-start(s32[2,256]{1,0:T(2,128)} %param.19) | copy-start | bytes 6148
  131.3 93.8 %copy-start.2 = (bf16[512,256]{1,0:T(8,128)(2,1)S(1)}, bf16[512,256]{1,0:T(8,128)(2,1)}, u32[]{:S(2)}) copy-start(bf16[512,256]{1,0:T(8,128)(2,1)} %copy-done.1) | copy-start | bytes 786436
  134.8 96.9 %all-to-all-start.2 = ((f32[32,32,256]{2,1,0:T(8,128)}), f32[32,32,256]{2,1,0:T(8,128)}, u32[]{:S(2)}, u32[]{:S(2)}) async-start(f32[32,32,256]{2,1,0:T(8,128)} %bitcast.331), calls=%async_computation.2 | async-start | bytes 2097152 | tf_op jit(solution)/shard_map/all_to_all | solution.py:256
  144.7 360.8 %all-reduce.3.cloned.1.call-start = ((), (), s32[]{:S(2)}) async-start(), calls=%async_computation.3 | async-start | bytes 4194304 | tf_op jit(solution)/shard_map/psum | solution.py:264
  230.9 0.7 copy-start.15
  231.0 347.0 %all-reduce.5.cloned.1.call-start = ((), (), s32[]{:S(2)}) async-start(), calls=%async_computation.4 | async-start | bytes 4194304 | tf_op jit(solution)/shard_map/psum | solution.py:265
  240.2 0.9 copy-start.8
  240.2 1.3 copy-start.11
  578.0 3.2 copy-start.4
Sparse Core Ops, SparseCore 0:
  84.9 27.1 all-gather.5
  231.1 274.2 all-reduce.2
  508.4 69.5 all-reduce.4
where the time goes:
time: 591 us; the launch traced here: 589 us
  waiting for transfers between devices  340 us (58%)
  blocking collectives  113 us (19%)
  other arithmetic  42.9 us (7%)
  local copies, waits for them, and re-layouts  32.7 us (6%)
  starting transfers between devices  27.6 us (5%)
  matrix products  17.2 us (3%)
  between operations  14.9 us (3%)
    psum x1, waiting for transfers between devices, body(): quot_grad = lax.psum(quot_part, ('user', 'hist'))  263 us
    psum x1, blocking collectives, body(): all_events = lax.psum(own_events, 'user')  79.2 us
    psum x1, waiting for transfers between devices, body(): rem_grad = lax.psum(rem_part, 'hist')  72.6 us
    all_gather x2, blocking collectives, carried_in_2(): lax.all_gather(part.astype(kind), axis)  25.3 us
  transfers between devices with their start and end apart: 6, of which 3 were waited for; matrix products, arithmetic and copies ran while one was open for 7% of the time, Pallas kernels for 0%

commit v1 on v0

--- a/solution.py
+++ b/solution.py
@@ -261,7 +261,7 @@
     )
     quot_part = grad_ratio * quot_part
     rem_part = grad_ratio * rem_part
-    quot_grad = lax.psum(quot_part, ("user", "hist"))
+    quot_grad = lax.psum(lax.psum(quot_part, "hist"), "user")
     rem_grad = lax.psum(rem_part, "hist")
     return (output, quot_grad, rem_grad)
 

time: 591 us -> 502 us (0.85)
  waiting for transfers between devices: 340 us -> 250 us
    psum x2, waiting for transfers between devices: 336 us -> 246 us  [body(): quot_grad = lax.psum(lax.psum(quot_part, 'hist'), 'user')]
  transfers between devices with their start and end apart: 6 -> 6, of which waited for: 3 -> 3; matrix products, arithmetic and copies ran while one was open for 7% -> 6% of each run, Pallas kernels for 0% -> 0%
where the time goes in v1:
time: 502 us; the launch traced here: 499 us
  waiting for transfers between devices  250 us (50%)
  blocking collectives  113 us (23%)
  other arithmetic  43.2 us (9%)
  local copies, waits for them, and re-layouts  31.4 us (6%)
  starting transfers between devices  27.3 us (5%)
  matrix products  17.2 us (3%)
  between operations  15 us (3%)
    psum x2, waiting for transfers between devices, body(): quot_grad = lax.psum(lax.psum(quot_part, 'hist'), 'user')  246 us
    psum x1, blocking collectives, body(): all_events = lax.psum(own_events, 'user')  79.2 us
    all_gather x2, blocking collectives, carried_in_2(): lax.all_gather(part.astype(kind), axis)  25.3 us
    all_to_all x1, starting transfers between devices, body(): lax.all_to_all(requests, 'user', split_axis=0, concat_axis=0, tiled=True)  11.7 us
  transfers between devices with their start and end apart: 6, of which 3 were waited for; matrix products, arithmetic and copies ran while one was open for 6% of the time, Pallas kernels for 0%

profile of v1, /device:TPU:8, one launch (start us, length us, event | category | flops | bytes accessed | tf_op | source)
XLA Modules:
  0.0 498.6 jit_solution(9446364104226246527)
XLA Ops:
  7.2 0.8 and_select_fusion.1
  8.0 0.7 copy.124
  8.7 0.7 copy.121
  9.4 1.2 reduce-window.14
  11.0 2.4 scatter_custom_fusion
  13.4 0.7 all_to_all.12
  14.1 11.7 %all-to-all-start = ((s32[32,1,32]{2,1,0:T(1,128)}), s32[32,1,32]{2,1,0:T(1,128)S(1)}, u32[]{:S(2)}, u32[]{:S(2)}) async-start(s32[32,1,32]{2,1,0:T(1,128)} %all_to_all.12), calls=%async_computation | async-start | bytes 32768 | tf_op jit(solution)/shard_map/all_to_all | solution.py:99
  25.8 0.7 reshape.410
  26.5 2.4 reduce-window.16
  29.6 0.7 fusion.87
  30.3 4.1 all-to-all-done
  35.1 3.9 gather_fusion.1
  39.0 1.0 broadcast_select_fusion
  40.0 5.7 %all-to-all-start.1 = ((bf16[32,32,256]{2,1,0:T(8,128)(2,1)}), bf16[32,32,256]{2,1,0:T(8,128)(2,1)S(1)}, u32[]{:S(2)}, u32[]{:S(2)}) async-start(bf16[32,32,256]{2,1,0:T(8,128)(2,1)} %broadcast_select_fusion), calls=%async_computation.1 | async-start | bytes 1048576 | tf_op jit(solution)/shard_map/all_to_all | solution.py:103
  45.9 10.6 %all-gather.3 = bf16[16,4,1]{1,2,0:T(2,128)(2,1)S(1)} all-gather(bf16[2,4,1]{1,2,0:T(2,128)(2,1)S(1)} %get-tuple-element.496), channel_id=5, replica_groups=mesh['user'=32,'hist'=8] {'hist'}, dimensions={0}, use_global_device_ids=true | all-gather | bytes 144 | tf_op jit(solution)/shard_map/all_gather | solution.py:26
  59.2 3.0 gather_fusion
  62.2 8.9 %all-gather = f32[16,4,1]{1,2,0:T(1,128)} all-gather(f32[2,4,1]{1,2,0:T(1,128)S(1)} %get-tuple-element.497), channel_id=2, replica_groups=mesh['user'=32,'hist'=8] {'hist'}, dimensions={0}, use_global_device_ids=true | all-gather | bytes 288 | tf_op jit(solution)/shard_map/all_gather | solution.py:12
  71.1 2.0 gather_fusion.2
  73.5 0.9 convert_multiply_fusion.5
  74.4 1.1 convolution_convert_fusion.2
  75.6 0.8 copy.88
  76.4 1.0 reshape.409
  77.5 1.7 convert_multiply_fusion.6
  79.1 1.1 convolution_convert_fusion.4
  80.3 1.0 reshape.489
  81.3 1.2 copy.95
  82.6 2.1 fusion.79
  85.1 14.8 %all-gather.2 = bf16[16,4,64,64]{3,2,1,0:T(8,128)(2,1)} all-gather(bf16[2,4,64,64]{3,2,1,0:T(8,128)(2,1)S(1)} %convolution_convert_fusion.5), channel_id=4, replica_groups=mesh['user'=32,'hist'=8] {'hist'}, dimensions={0}, use_global_device_ids=true | all-gather | bytes 589824 | tf_op jit(solution)/shard_map/all_gather | solution.py:26
  99.9 13.5 %while.57 = (s32[]{:T(128)}, f32[2,4,64,64]{3,2,1,0:T(8,128)S(1)}, s32[]{:T(128)}, bf16[8,2,4]{2,1,0:T(2,128)(2,1)}, bf16[8,2,4,64,64]{4,3,2,1,0:T(8,128)(2,1)},...) while((s32[]{:T(128)}, f32[2,4,64,64]{3,2,1,0:T(8,128)S(1)}, s32[]{:T(128)}, ...), condition=%wide.region_13.14_spmd.clone, body=%wide.region_12.13_spmd.clone.sunk | while | flops 163856 | bytes 327935 | solution.py:44
  99.9 0.7 bitcast_convert_fusion.2
  100.6 1.0 fusion.168
  102.3 1.0 fusion.168
  103.9 1.0 fusion.168
  105.7 1.0 fusion.168
  107.3 1.0 fusion.168
  109.1 1.0 fusion.168
  110.1 0.7 bitcast_convert_fusion.2
  110.8 1.0 fusion.168
  112.4 1.0 fusion.168
  113.7 4.2 while.55
  113.8 1.3 bitcast_dynamic-update-slice_fusion.2
  115.9 1.3 bitcast_dynamic-update-slice_fusion.2
  118.0 0.7 copy-done.7
  118.7 0.7 broadcast.273
  119.4 9.1 %while.56 = (s32[]{:T(128)}, bf16[2,256,4,64]{1,3,2,0:T(8,128)(2,1)}, bf16[2,256,4,64]{1,3,2,0:T(8,128)(2,1)S(1)}, bf16[2,256,4,64]{1,3,2,0:T(8,128)(2,1)S(1)}, ...) while((s32[]{:T(128)}, ...), condition=%wide.region_15.16_spmd, body=%wide.region_14.15_spmd.sunk | while | flops 287442944 | bytes 7786197 | solution.py:220
  119.4 0.7 multiply_bitcast_fusion.3
  120.7 1.3 fusion.167
  123.3 0.7 copy-done.6
  124.0 0.7 multiply_bitcast_fusion.3
  125.3 1.3 fusion.167
  127.9 0.7 copy-done.6
  128.9 1.2 copy.108
  131.4 3.5 scatter_custom_fusion.2
  134.9 9.8 %all-to-all-start.2 = ((f32[32,32,256]{2,1,0:T(8,128)}), f32[32,32,256]{2,1,0:T(8,128)}, u32[]{:S(2)}, u32[]{:S(2)}) async-start(f32[32,32,256]{2,1,0:T(8,128)} %bitcast.331), calls=%async_computation.2 | async-start | bytes 2097152 | tf_op jit(solution)/shard_map/all_to_all | solution.py:256
  145.4 79.2 %psum.28 = f32[]{:T(128)} all-reduce(f32[]{:T(128)} %convert_reduce_fusion), channel_id=1, replica_groups=mesh['user'=32,'hist'=8] {'user'}, use_global_device_ids=true, to_apply=%region_11.12 | all-reduce | flops 1 | bytes 8 | tf_op jit(solution)/shard_map/psum | solution.py:83
  225.4 4.6 scatter_custom_fusion.1
  230.0 1.5 broadcast_multiply_fusion.1
  231.4 7.0 %scatter_custom_fusion.3 = f32[2048,256]{1,0:T(8,128)S(1)} fusion(s32[1024]{0:T(1024)S(1)} %reshape.473, f32[1024,256]{1,0:T(8,128)} %bitcast.52, f32[]{:T(128)} %constant.162.clone.1), kind=kCustom, calls=%fused_computation.108 | custom fusion | flops 262144 | bytes 2097664 | tf_op jit(solution)/shard_map/scatter-add | solution.py:259
  238.5 1.5 broadcast_multiply_fusion
  240.0 91.1 %all-reduce.6.cloned.1.call-done = (f32[2048,256]{1,0:T(8,128)}, f32[2048,256]{1,0:T(8,128)}) async-done(((f32[2048,256]{1,0:T(8,128)}, f32[2048,256]{1,0:T(8,128)}), (f32[2048,256]{1,0:T(8,128)}, f32[2048,256]{1,0:T(8,128)})) %all-reduce.6.cloned.1.call-update) | async-done | bytes 4194320 | tf_op jit(solution)/shard_map/psum | solution.py:264
  331.5 1.0 convolution_convert_fusion.1
  332.4 155.1 %all-reduce.4.cloned.1.call-done = f32[2048,256]{1,0:T(8,128)} async-done(((f32[2048,256]{1,0:T(8,128)}), f32[2048,256]{1,0:T(8,128)}) %all-reduce.4.cloned.1.call-update) | async-done | bytes 2097168 | tf_op jit(solution)/shard_map/psum | solution.py:264
  487.6 3.2 copy.178
  490.8 1.3 copy.179
  (147 shorter events, 17.5 us)
Async XLA Ops:
  7.2 27.9 %copy-start = (bf16[2048,256]{1,0:T(8,128)(2,1)S(1)}, bf16[2048,256]{1,0:T(8,128)(2,1)}, u32[]{:S(2)}) copy-start(bf16[2048,256]{1,0:T(8,128)(2,1)} %param.24) | copy-start | bytes 3145732
  11.0 60.1 %copy-start.18 = (s32[512,1]{0,1:T(1,128)}, s32[512,1]{0,1:T(1,128)S(1)}, u32[]{:S(2)}) copy-start(s32[512,1]{0,1:T(1,128)S(1)} %compare_select_fusion.1) | copy-start | bytes 6148
  14.1 20.3 %all-to-all-start = ((s32[32,1,32]{2,1,0:T(1,128)}), s32[32,1,32]{2,1,0:T(1,128)S(1)}, u32[]{:S(2)}, u32[]{:S(2)}) async-start(s32[32,1,32]{2,1,0:T(1,128)} %all_to_all.12), calls=%async_computation | async-start | bytes 32768 | tf_op jit(solution)/shard_map/all_to_all | solution.py:99
  39.0 6.8 %copy-start.19 = (s32[2]{0:T(128)S(1)}, s32[2]{0:T(128)}, u32[]{:S(2)}) copy-start(s32[2]{0:T(128)} %param.21) | copy-start | bytes 28
  39.0 6.9 %copy-start.16 = (s32[2,256]{1,0:T(2,128)S(1)}, s32[2,256]{1,0:T(2,128)}, u32[]{:S(2)}) copy-start(s32[2,256]{1,0:T(2,128)} %param.19) | copy-start | bytes 6148
  39.0 19.2 %copy-start.14 = (bf16[2,256,256]{2,1,0:T(8,128)(2,1)S(1)}, bf16[2,256,256]{2,1,0:T(8,128)(2,1)}, u32[]{:S(2)}) copy-start(bf16[2,256,256]{2,1,0:T(8,128)(2,1)} %param.29) | copy-start | bytes 786436
  39.0 19.3 %copy-start.10 = (bf16[256,256]{1,0:T(8,128)(2,1)S(1)}, bf16[256,256]{1,0:T(8,128)(2,1)}, u32[]{:S(2)}) copy-start(bf16[256,256]{1,0:T(8,128)(2,1)} %param.28) | copy-start | bytes 393220
  40.0 31.0 %all-to-all-start.1 = ((bf16[32,32,256]{2,1,0:T(8,128)(2,1)}), bf16[32,32,256]{2,1,0:T(8,128)(2,1)S(1)}, u32[]{:S(2)}, u32[]{:S(2)}) async-start(bf16[32,32,256]{2,1,0:T(8,128)(2,1)} %broadcast_select_fusion), calls=%async_computation.1 | async-start | bytes 1048576 | tf_op jit(solution)/shard_map/all_to_all | solution.py:103
  45.7 67.7 %all-gather.6.cloned.1.call-start = ((), (), s32[]{:S(2)}) async-start(), calls=%async_computation.4 | async-start | bytes 2359296 | tf_op jit(solution)/shard_map/all_gather | solution.py:12
  59.2 13.9 %copy-start.9 = (bf16[256,256]{1,0:T(8,128)(2,1)S(1)}, bf16[256,256]{1,0:T(8,128)(2,1)}, u32[]{:S(2)}) copy-start(bf16[256,256]{1,0:T(8,128)(2,1)} %param.25) | copy-start | bytes 393220
  73.0 6.1 %copy-start.1 = (bf16[512,256]{1,0:T(8,128)(2,1)}, bf16[512,256]{1,0:T(8,128)(2,1)S(1)}, u32[]{:S(2)}) copy-start(bf16[512,256]{1,0:T(8,128)(2,1)S(1)} %gather_fusion.2) | copy-start | bytes 786436
  117.9 0.7 copy-start.7
  122.0 1.0 copy-start.5
  123.3 0.7 copy-start.6
  126.6 1.0 copy-start.5
  127.9 0.7 copy-start.6
  128.6 2.2 copy-start.12
  130.1 0.9 copy-start.13
  131.3 94.1 %copy-start.3 = (f32[512,256]{1,0:T(8,128)}, f32[512,256]{1,0:T(8,128)S(1)}, u32[]{:S(2)}) copy-start(f32[512,256]{1,0:T(8,128)S(1)} %convolution_add_fusion) | copy-start | bytes 1572868
  131.3 13.4 %copy-start.20 = (s32[2]{0:T(128)S(1)}, s32[2]{0:T(128)}, u32[]{:S(2)}) copy-start(s32[2]{0:T(128)} %param.21) | copy-start | bytes 28
  131.3 93.3 %copy-start.17 = (s32[2,256]{1,0:T(2,128)S(1)}, s32[2,256]{1,0:T(2,128)}, u32[]{:S(2)}) copy-start(s32[2,256]{1,0:T(2,128)} %param.19) | copy-start | bytes 6148
  131.3 94.0 %copy-start.15 = (s32[32,1,32]{2,0,1:T(8,128)S(1)}, s32[32,1,32]{2,0,1:T(8,128)}, u32[]{:S(2)}) copy-start(s32[32,1,32]{2,0,1:T(8,128)} %get-tuple-element.487) | copy-start | bytes 12292
  131.4 94.0 %copy-start.2 = (bf16[512,256]{1,0:T(8,128)(2,1)S(1)}, bf16[512,256]{1,0:T(8,128)(2,1)}, u32[]{:S(2)}) copy-start(bf16[512,256]{1,0:T(8,128)(2,1)} %copy-done.1) | copy-start | bytes 786436
  134.9 96.5 %all-to-all-start.2 = ((f32[32,32,256]{2,1,0:T(8,128)}), f32[32,32,256]{2,1,0:T(8,128)}, u32[]{:S(2)}, u32[]{:S(2)}) async-start(f32[32,32,256]{2,1,0:T(8,128)} %bitcast.331), calls=%async_computation.2 | async-start | bytes 2097152 | tf_op jit(solution)/shard_map/all_to_all | solution.py:256
  144.7 186.4 %all-reduce.6.cloned.1.call-start = ((), (), s32[]{:S(2)}) async-start(), calls=%async_computation.5 | async-start | bytes 8388608 | tf_op jit(solution)/shard_map/psum | solution.py:264
  240.0 91.2 %copy-start.8 = (bf16[2,256,4,64]{1,3,2,0:T(8,128)(2,1)S(1)}, bf16[2,256,4,64]{1,3,2,0:T(8,128)(2,1)}, u32[]{:S(2)}) copy-start(bf16[2,256,4,64]{1,3,2,0:T(8,128)(2,1)} %copy-done.7) | copy-start | bytes 786436
  240.0 91.5 %copy-start.11 = (bf16[256,256]{1,0:T(8,128)(2,1)S(1)}, bf16[256,256]{1,0:T(8,128)(2,1)}, u32[]{:S(2)}) copy-start(bf16[256,256]{1,0:T(8,128)(2,1)} %param.28) | copy-start | bytes 393220
  240.0 247.6 %all-reduce.4.cloned.1.call-start = ((), (), s32[]{:S(2)}) async-start(), calls=%async_computation.3 | async-start | bytes 4194304 | tf_op jit(solution)/shard_map/psum | solution.py:264
  487.6 3.2 copy-start.4
Sparse Core Ops, SparseCore 0:
  84.9 27.3 all-gather.5
  240.1 90.9 all-reduce.5
  334.6 152.8 all-reduce.3
